TPU v7x, 512 devices: a whole 4x8x8 slice. The times are simulated.
512 devices in a mesh: section: 16 (over z, core), expert: 32 (over x, y).
Axes of the slice: x: 4, y: 8, z: 8, core: 2. Of those that a mesh axis runs over, the one named last changes fastest.
Arguments:
- state: bfloat16 [2, 16, 1024, 3584], P(None, 'section', 'expert'), may hold values from -6 to 6
- fresh: bfloat16 [2, 1024, 3584], P(None, 'expert'), may hold values from -6 to 6
- norm_gain: float32 [16, 3584], P('section'), may hold values from 0.5 to 1.5
- w_gate: bfloat16 [16, 3584, 4096], P('section', None, 'expert'), may hold values from -0.09375 to 0.09375
- w_up: bfloat16 [16, 3584, 4096], P('section', None, 'expert'), may hold values from -0.09375 to 0.09375
- w_down: bfloat16 [16, 4096, 3584], P('section', 'expert'), may hold values from -0.1875 to 0.1875
- routes: int32 [2, 2, 16, 1024, 2], P(None, None, 'section', 'expert'), may hold values from 0 to 3, all different within a row; in each aligned block of 32 rows (0 to 31, 32 to 63, ..., all dimensions but the last counted through in order) at most 18 rows name the same one
- gates: float32 [2, 2, 16, 1024, 2], P(None, None, 'section', 'expert'), may hold values from 0.1 to 1
Outputs:
- advanced: bfloat16 [2, 16, 1024, 3584], P(None, 'section', 'expert')
Inputs may be any that keep to these rules, and one draw needn't show every extreme that they name: `routes`: each row names 2 different experts. In each aligned block of 32 rows (one device's rows of one tick, direction and section) no expert is named by more than 18 rows, and in some blocks one is named by exactly 18.
All inputs are finite; a program needn't handle non-finite values.
Results may differ from a plain program's by a relative error of at most 0.007.
Values may be sent and summed in bfloat16 or wider, within the bound.
A program may use at most 128 MiB of HBM per device.

v0:
```python
import jax
import jax.numpy as jnp
from jax import lax
from jax.sharding import PartitionSpec as P

EXPERTS = 4
CAP = 18


def shifted(array, axis, by):
    peers = lax.axis_size(axis)
    pairs = [(i, i + by) for i in range(peers) if 0 <= i + by < peers]
    return lax.ppermute(array, axis, pairs)


def build_slots(route_ids):
    is_hit = jnp.any(route_ids[..., None] == jnp.arange(EXPERTS, dtype=jnp.int32), axis=-2)
    slot_rank = jnp.cumsum(is_hit.astype(jnp.int32), axis=-2) - 1
    return is_hit[..., None] & (slot_rank[..., None] == jnp.arange(CAP, dtype=jnp.int32))


def expert_rows(slot_rows, gate_up, down_w):
    width = slot_rows.shape[-1]
    hid_count = down_w.shape[0]
    flat_rows = slot_rows.reshape(-1, width)
    joined = jnp.dot(flat_rows, gate_up, preferred_element_type=jnp.float32)
    hidden = (jax.nn.silu(joined[:, :hid_count]) * joined[:, hid_count:]).astype(jnp.bfloat16)
    partials = jnp.dot(hidden, down_w, preferred_element_type=jnp.float32).astype(jnp.bfloat16)
    return partials.reshape(slot_rows.shape)


def send_back(partials):
    return lax.all_to_all(partials, "expert", split_axis=0, concat_axis=0, tiled=True)


def moe_layer(inputs, route_ids, route_wts, norm_scale, gate_up, down_w):
    device_count = lax.axis_size("expert")
    group_size = device_count // EXPERTS
    x_wide = inputs.astype(jnp.float32)
    mean_sq = jnp.mean(x_wide * x_wide, axis=-1, keepdims=True)
    normed = (x_wide * lax.rsqrt(mean_sq + 1e-06) * norm_scale).astype(jnp.bfloat16)
    slot_map = build_slots(route_ids)
    wide_map = jnp.repeat(slot_map.astype(jnp.bfloat16), group_size, axis=2)
    outgoing = jnp.einsum(
        "rnjc,rnd->jrcd", wide_map, normed, preferred_element_type=jnp.float32
    ).astype(jnp.bfloat16)
    returned = send_back(
        expert_rows(
            lax.all_to_all(outgoing, "expert", split_axis=0, concat_axis=0, tiled=True),
            gate_up,
            down_w,
        )
    )
    expert_hit = route_ids[..., None] == jnp.arange(EXPERTS, dtype=jnp.int32)
    weight = jnp.sum(jnp.where(expert_hit, route_wts[..., None], jnp.float32(0.0)), axis=2)
    combine_wt = slot_map.astype(jnp.float32) * weight[..., None]
    wide_wt = jnp.repeat(combine_wt, group_size, axis=2)
    mixed_sum = jnp.einsum(
        "rnjc,jrcd->rnd", wide_wt, returned.astype(jnp.float32), precision=lax.Precision.HIGHEST
    )
    return (x_wide + mixed_sum).astype(jnp.bfloat16)


def per_device(state, fresh, norm_gain, w_gate, w_up, w_down, routes, gates):
    norm_scale = norm_gain[0]
    gate_up = jnp.concatenate([w_gate[0], w_up[0]], axis=1)
    down_w = w_down[0]

    def both_layers(inputs, route_ids, route_wts):
        forward_out = moe_layer(
            inputs[0:1], route_ids[0:1], route_wts[0:1], norm_scale, gate_up, down_w
        )
        reverse_out = moe_layer(
            inputs[1:2], route_ids[1:2], route_wts[1:2], norm_scale, gate_up, down_w
        )
        return jnp.concatenate([forward_out, reverse_out], axis=0)

    first_out = both_layers(state[:, 0], routes[0, :, 0], gates[0, :, 0])
    onward = shifted(first_out[0], "section", 1)
    backward = shifted(first_out[1], "section", -1)
    position = lax.axis_index("section")
    last_section = lax.axis_size("section") - 1
    input_fwd = jnp.where(position == 0, fresh[0], onward)
    input_rev = jnp.where(position == last_section, fresh[1], backward)
    second = both_layers(jnp.stack([input_fwd, input_rev], axis=0), routes[1, :, 0], gates[1, :, 0])
    return second[:, None]


def solution(mesh):
    in_specs = (
        P(None, "section", "expert", None),
        P(None, "expert", None),
        P("section", None),
        P("section", None, "expert"),
        P("section", None, "expert"),
        P("section", "expert", None),
        P(None, None, "section", "expert", None),
        P(None, None, "section", "expert", None),
    )
    out_specs = P(None, "section", "expert", None)
    return jax.shard_map(
        per_device, mesh=mesh, in_specs=in_specs, out_specs=out_specs, check_vma=False
    )
```

profile of v0, /device:TPU:249, one launch (start us, length us, event | category | flops | bytes accessed | tf_op | source)
XLA Modules:
  0.0 1095.8 jit_solution(8199837720199635491)
XLA Ops:
  5.3 4.7 copy.102
  10.0 9.1 all-to-all-start.4
  20.7 4.7 copy.90
  25.4 118.4 %all-to-all-done.4 = bf16[32,1,18,3584]{3,2,1,0:T(8,128)(2,1)} async-done(((bf16[32,1,18,3584]{3,2,1,0:T(8,128)(2,1)}), bf16[32,1,18,3584]{3,2,1,0:T(8,128)(2,1)}, u32[]{:S(2)}, u32[]{:S(2)}) %all-to-all-start.4) | async-done | bytes 4128800 | tf_op jit(solution)/shard_map/all_to_all | solution.py:49
  143.7 6.8 all-to-all-start
  150.6 7.4 reshape.497
  164.8 7.3 reshape.498
  172.1 102.7 %all-to-all-done = bf16[32,1,18,3584]{3,2,1,0:T(8,128)(2,1)} async-done(((bf16[32,1,18,3584]{3,2,1,0:T(8,128)(2,1)}), bf16[32,1,18,3584]{3,2,1,0:T(8,128)(2,1)}, u32[]{:S(2)}, u32[]{:S(2)}) %all-to-all-start) | async-done | bytes 4128800 | tf_op jit(solution)/shard_map/all_to_all | solution.py:49
  274.9 7.2 all-to-all-start.5
  282.1 7.3 reshape.491
  296.3 7.2 reshape.492
  303.5 103.2 %all-to-all-done.5 = bf16[32,1,18,3584]{3,2,1,0:T(8,128)(2,1)} async-done(((bf16[32,1,18,3584]{3,2,1,0:T(8,128)(2,1)}), bf16[32,1,18,3584]{3,2,1,0:T(8,128)(2,1)}, u32[]{:S(2)}, u32[]{:S(2)}) %all-to-all-start.5) | async-done | bytes 4128800 | tf_op jit(solution)/shard_map/all_to_all | solution.py:33
  406.7 6.3 all-to-all-start.1
  413.3 5.5 fusion.10
  421.8 116.1 %all-to-all-done.1 = bf16[32,1,18,3584]{3,2,1,0:T(8,128)(2,1)} async-done(((bf16[32,1,18,3584]{3,2,1,0:T(8,128)(2,1)}), bf16[32,1,18,3584]{3,2,1,0:T(8,128)(2,1)}, u32[]{:S(2)}, u32[]{:S(2)}) %all-to-all-start.1) | async-done | bytes 4128800 | tf_op jit(solution)/shard_map/all_to_all | solution.py:33
  537.9 5.4 fusion.8
  543.3 5.8 collective-permute-start
  553.4 4.7 copy.96
  558.1 6.3 all-to-all-start.2
  570.6 120.4 %all-to-all-done.2 = bf16[32,1,18,3584]{3,2,1,0:T(8,128)(2,1)} async-done(((bf16[32,1,18,3584]{3,2,1,0:T(8,128)(2,1)}), bf16[32,1,18,3584]{3,2,1,0:T(8,128)(2,1)}, u32[]{:S(2)}, u32[]{:S(2)}) %all-to-all-start.2) | async-done | bytes 4128800 | tf_op jit(solution)/shard_map/all_to_all | solution.py:49
  690.9 11.0 %all-to-all-start.6 = ((bf16[32,1,18,3584]{3,2,1,0:T(8,128)(2,1)}), bf16[32,1,18,3584]{3,2,1,0:T(8,128)(2,1)}, u32[]{:S(2)}, u32[]{:S(2)}) async-start(bf16[32,1,18,3584]{3,2,1,0:T(8,128)(2,1)} %copy.108), calls=%async_computation.6 | async-start | bytes 11010048 | tf_op jit(solution)/shard_map/all_to_all | solution.py:49
  701.9 7.4 reshape.494
  716.2 7.3 reshape.495
  723.5 103.6 %all-to-all-done.6 = bf16[32,1,18,3584]{3,2,1,0:T(8,128)(2,1)} async-done(((bf16[32,1,18,3584]{3,2,1,0:T(8,128)(2,1)}), bf16[32,1,18,3584]{3,2,1,0:T(8,128)(2,1)}, u32[]{:S(2)}, u32[]{:S(2)}) %all-to-all-start.6) | async-done | bytes 4128800 | tf_op jit(solution)/shard_map/all_to_all | solution.py:49
  827.1 6.5 all-to-all-start.3
  833.6 7.3 reshape.500
  847.8 7.2 reshape.501
  855.0 103.2 %all-to-all-done.3 = bf16[32,1,18,3584]{3,2,1,0:T(8,128)(2,1)} async-done(((bf16[32,1,18,3584]{3,2,1,0:T(8,128)(2,1)}), bf16[32,1,18,3584]{3,2,1,0:T(8,128)(2,1)}, u32[]{:S(2)}, u32[]{:S(2)}) %all-to-all-start.3) | async-done | bytes 4128800 | tf_op jit(solution)/shard_map/all_to_all | solution.py:33
  958.2 6.4 all-to-all-start.7
  964.6 5.4 fusion.13
  970.1 119.3 %all-to-all-done.7 = bf16[32,1,18,3584]{3,2,1,0:T(8,128)(2,1)} async-done(((bf16[32,1,18,3584]{3,2,1,0:T(8,128)(2,1)}), bf16[32,1,18,3584]{3,2,1,0:T(8,128)(2,1)}, u32[]{:S(2)}, u32[]{:S(2)}) %all-to-all-start.7) | async-done | bytes 4128800 | tf_op jit(solution)/shard_map/all_to_all | solution.py:33
  1089.4 5.4 fusion.12
  (71 shorter events, 48.8 us)
Async XLA Ops:
  0.0 161.6 %copy-start = (bf16[1,128,3584]{2,1,0:T(8,128)(2,1)S(1)}, bf16[1,128,3584]{2,1,0:T(8,128)(2,1)}, u32[]{:S(2)}) copy-start(bf16[1,128,3584]{2,1,0:T(8,128)(2,1)} %param.13) | copy-start | bytes 2752516
  10.0 9.4 copy-start.1
  10.0 133.7 %all-to-all-start.4 = ((bf16[32,1,18,3584]{3,2,1,0:T(8,128)(2,1)}), bf16[32,1,18,3584]{3,2,1,0:T(8,128)(2,1)}, u32[]{:S(2)}, u32[]{:S(2)}) async-start(bf16[32,1,18,3584]{3,2,1,0:T(8,128)(2,1)} %copy.102), calls=%async_computation.4 | async-start | bytes 11010048 | tf_op jit(solution)/shard_map/all_to_all | solution.py:49
  143.7 131.1 %all-to-all-start = ((bf16[32,1,18,3584]{3,2,1,0:T(8,128)(2,1)}), bf16[32,1,18,3584]{3,2,1,0:T(8,128)(2,1)}, u32[]{:S(2)}, u32[]{:S(2)}) async-start(bf16[32,1,18,3584]{3,2,1,0:T(8,128)(2,1)} %copy.90), calls=%async_computation | async-start | bytes 11010048 | tf_op jit(solution)/shard_map/all_to_all | solution.py:49
  150.6 7.4 copy-start.4
  274.9 131.9 %all-to-all-start.5 = ((bf16[32,1,18,3584]{3,2,1,0:T(8,128)(2,1)}), bf16[32,1,18,3584]{3,2,1,0:T(8,128)(2,1)}, u32[]{:S(2)}, u32[]{:S(2)}) async-start(bf16[32,1,18,3584]{3,2,1,0:T(8,128)(2,1)} %bitcast.155), calls=%async_computation.5 | async-start | bytes 11010048 | tf_op jit(solution)/shard_map/all_to_all | solution.py:33
  406.7 6.5 copy-start.3
  406.7 131.1 %all-to-all-start.1 = ((bf16[32,1,18,3584]{3,2,1,0:T(8,128)(2,1)}), bf16[32,1,18,3584]{3,2,1,0:T(8,128)(2,1)}, u32[]{:S(2)}, u32[]{:S(2)}) async-start(bf16[32,1,18,3584]{3,2,1,0:T(8,128)(2,1)} %bitcast.153), calls=%async_computation.1 | async-start | bytes 11010048 | tf_op jit(solution)/shard_map/all_to_all | solution.py:33
  413.3 138.5 %copy-start.2 = (bf16[2,32,3584]{2,1,0:T(8,128)(2,1)S(1)}, bf16[2,32,3584]{2,1,0:T(8,128)(2,1)}, u32[]{:S(2)}) copy-start(bf16[2,32,3584]{2,1,0:T(8,128)(2,1)} %param.9) | copy-start | bytes 1376260
  418.8 130.4 %collective-permute-start.1 = (bf16[32,3584]{1,0:T(8,128)(2,1)S(1)}, bf16[32,3584]{1,0:T(8,128)(2,1)S(1)}, u32[]{:S(2)}, u32[]{:S(2)}) collective-permute-start(bf16[32,3584]{1,0:T(8,128)(2,1)S(1)} %fusion.10), channel_id=1, source_target_pairs={{32,0},{64,32},{96,64},{128,96},{160,128},{192,160},{224,192},{256... | collective-permute-start | bytes 688136 | tf_op jit(solution)/shard_map/ppermute | solution.py:13
  543.3 8.5 collective-permute-start
  558.1 132.8 %all-to-all-start.2 = ((bf16[32,1,18,3584]{3,2,1,0:T(8,128)(2,1)}), bf16[32,1,18,3584]{3,2,1,0:T(8,128)(2,1)}, u32[]{:S(2)}, u32[]{:S(2)}) async-start(bf16[32,1,18,3584]{3,2,1,0:T(8,128)(2,1)} %copy.96), calls=%async_computation.2 | async-start | bytes 11010048 | tf_op jit(solution)/shard_map/all_to_all | solution.py:49
  690.9 136.1 %all-to-all-start.6 = ((bf16[32,1,18,3584]{3,2,1,0:T(8,128)(2,1)}), bf16[32,1,18,3584]{3,2,1,0:T(8,128)(2,1)}, u32[]{:S(2)}, u32[]{:S(2)}) async-start(bf16[32,1,18,3584]{3,2,1,0:T(8,128)(2,1)} %copy.108), calls=%async_computation.6 | async-start | bytes 11010048 | tf_op jit(solution)/shard_map/all_to_all | solution.py:49
  701.9 7.4 copy-start.5
  827.1 131.1 %all-to-all-start.3 = ((bf16[32,1,18,3584]{3,2,1,0:T(8,128)(2,1)}), bf16[32,1,18,3584]{3,2,1,0:T(8,128)(2,1)}, u32[]{:S(2)}, u32[]{:S(2)}) async-start(bf16[32,1,18,3584]{3,2,1,0:T(8,128)(2,1)} %bitcast.156), calls=%async_computation.3 | async-start | bytes 11010048 | tf_op jit(solution)/shard_map/all_to_all | solution.py:33
  958.2 131.2 %all-to-all-start.7 = ((bf16[32,1,18,3584]{3,2,1,0:T(8,128)(2,1)}), bf16[32,1,18,3584]{3,2,1,0:T(8,128)(2,1)}, u32[]{:S(2)}, u32[]{:S(2)}) async-start(bf16[32,1,18,3584]{3,2,1,0:T(8,128)(2,1)} %bitcast.154), calls=%async_computation.7 | async-start | bytes 11010048 | tf_op jit(solution)/shard_map/all_to_all | solution.py:33
where the time goes:
time: 1110 us; the launch traced here: 1100 us
  waiting for transfers between devices  889 us (80%)
  local copies, waits for them, and re-layouts  78.7 us (7%)
  starting transfers between devices  68.3 us (6%)
  matrix products  55.1 us (5%)
    all_to_all x4, waiting for transfers between devices, moe_layer(): lax.all_to_all(outgoing, 'expert', split_axis=0, concat_axis=0, tiled=True)  445 us
    all_to_all x4, waiting for transfers between devices, send_back(): lax.all_to_all(partials, 'expert', split_axis=0, concat_axis=0, tiled=True)  442 us
    all_to_all x4, starting transfers between devices, moe_layer(): lax.all_to_all(outgoing, 'expert', split_axis=0, concat_axis=0, tiled=True)  33.2 us
    reshape x4, local copies, waits for them, and re-layouts, expert_rows(): flat_rows = slot_rows.reshape(-1, width)  29.5 us
    reshape x4, local copies, waits for them, and re-layouts, expert_rows(): return partials.reshape(slot_rows.shape)  29 us
    all_to_all x4, starting transfers between devices, send_back(): lax.all_to_all(partials, 'expert', split_axis=0, concat_axis=0, tiled=True)  26.4 us
  transfers between devices with their start and end apart: 10, of which 9 were waited for; matrix products, arithmetic and copies ran while one was open for 10% of the time, Pallas kernels for 0%

commit v1 on v0

v1 whole, which is shorter than its diff:
```python
import functools

import jax
import jax.numpy as jnp
from jax import lax
from jax.experimental import pallas as pl
from jax.experimental.pallas import tpu as pltpu
from jax.sharding import PartitionSpec as P

MESH = pl.DeviceIdType.MESH
NX, NY = 4, 8
ROWS = 32
HALF = ROWS // 2
D = 3584
HID = 128
NC = 4
COLS = D // NC
NQ = 4
QROWS = D // NQ
N_SEMS = 240
F32, BF16 = jnp.float32, jnp.bfloat16


def kernel(n_section, state, fresh, gain, w_gate, w_up, w_down, routes, gates, out,
           wgu, wd, xn, hid, part, rsb, snd, xs, xin, cw, send_sem, recv_sem, local_sem):
    expert = lax.axis_index("expert")
    section = lax.axis_index("section")
    ix, iy = expert // NY, expert % NY

    def along(dx, dy):
        return {"expert": ((ix + dx + NX) % NX) * NY + (iy + dy + NY) % NY}

    right, left = along(0, 1), along(0, -1)
    x_right, x_left = along(1, 0), along(-1, 0)
    onward = {"section": (section + 1) % n_section}
    backward = {"section": (section + n_section - 1) % n_section}

    count = [0]
    sent = []

    def copy_to(src, dst, device):
        at = count[0]
        count[0] += 1
        copy = pltpu.make_async_remote_copy(
            src_ref=src, dst_ref=dst, send_sem=send_sem.at[at], recv_sem=recv_sem.at[at],
            device_id=device, device_id_type=MESH)
        sent.append(copy)
        return copy

    barrier = pltpu.get_barrier_semaphore()
    for peer in (right, left, x_right, x_left, onward, backward):
        pl.semaphore_signal(barrier, inc=1, device_id=peer, device_id_type=MESH)

    own = []
    for q in range(NQ):
        rows = pl.ds(q * QROWS, QROWS)
        own.append((
            pltpu.make_async_copy(w_gate.at[0, rows], wgu.at[0, rows, pl.ds(0, HID)], local_sem.at[2 * q]),
            pltpu.make_async_copy(w_up.at[0, rows], wgu.at[0, rows, pl.ds(HID, HID)], local_sem.at[2 * q + 1])))
    own_wd = pltpu.make_async_copy(w_down.at[0], wd.at[pl.ds(0, HID)], local_sem.at[2 * NQ])
    for q in (0, 2, 1, 3):
        own[q][0].start()
        own[q][1].start()
    own_wd.start()

    def normed(x):
        wide = x.astype(F32)
        mean_sq = jnp.mean(wide * wide, axis=-1, keepdims=True)
        return (wide * lax.rsqrt(mean_sq + 1e-06) * gain[...]).astype(BF16)

    def slot(s, half=None):
        if half is None:
            return pl.ds(s * ROWS, ROWS)
        return pl.ds(s * ROWS + half * HALF, HALF)

    for d in range(2):
        xn[0, d, slot(0)] = normed(state[d, 0])

    column_expert = (ix + NX - lax.broadcasted_iota(jnp.int32, (ROWS, 128), 1) % NX) % NX
    for t in range(2):
        for d in range(2):
            ids, wts = routes[t, d, 0], gates[t, d, 0]
            cw[0, pl.ds((t * 2 + d) * ROWS, ROWS)] = (
                jnp.where(ids[:, 0:1] == column_expert, wts[:, 0:1], 0.0)
                + jnp.where(ids[:, 1:2] == column_expert, wts[:, 1:2], 0.0))

    pl.semaphore_wait(barrier, 6)

    def q_rows(q):
        return pl.ds(q * QROWS, QROWS)

    gu_r = [copy_to(wgu.at[0, q_rows(q)], wgu.at[1, q_rows(q)], x_right) for q in range(NQ)]
    gu_l = [copy_to(wgu.at[0, q_rows(q)], wgu.at[3, q_rows(q)], x_left) for q in range(NQ)]
    gu_fr = {q: copy_to(wgu.at[1, q_rows(q)], wgu.at[2, q_rows(q)], x_right) for q in (0, 1)}
    gu_fl = {q: copy_to(wgu.at[3, q_rows(q)], wgu.at[2, q_rows(q)], x_left) for q in (2, 3)}

    def cols(c):
        return pl.ds(c * COLS, COLS)

    def wd_at(r, c, half=None):
        if half is None:
            return wd.at[pl.ds(r * HID, HID), cols(c)]
        return wd.at[pl.ds(r * HID + half * (HID // 2), HID // 2), cols(c)]

    wd_r = [copy_to(wd_at(0, c), wd_at(1, c), x_right) for c in range(NC)]
    wd_l = [copy_to(wd_at(0, c), wd_at(3, c), x_left) for c in range(NC)]
    wd_fr = [copy_to(wd_at(1, c, 0), wd_at(2, c, 0), x_right) for c in range(NC)]
    wd_fl = [copy_to(wd_at(3, c, 1), wd_at(2, c, 1), x_left) for c in range(NC)]

    def gather(t, d):
        ring = []
        for h in range(4):
            a, b = (0, 1) if h == 3 else (None, None)
            ring.append((
                copy_to(xn.at[t, d, slot(h, a)], xn.at[t, d, slot(h + 1, a)], right),
                copy_to(xn.at[t, d, slot((8 - h) % 8, b)], xn.at[t, d, slot(7 - h, b)], left)))
        return ring

    ag = [[gather(t, d) for d in range(2)] for t in range(2)]

    def ag_hop(t, d, h):
        for side in range(2):
            if h > 0:
                ag[t][d][h - 1][side].wait_recv()
            if h < 4:
                ag[t][d][h][side].start()

    cw_ring = [(copy_to(cw.at[h], cw.at[h + 1], right),
                copy_to(cw.at[(8 - h) % 8], cw.at[7 - h], left) if h < 3 else None) for h in range(4)]

    def gate_up(t, d, r):
        joined = jnp.dot(xn[t, d], wgu[r], preferred_element_type=F32)
        g, u = joined[:, :HID], joined[:, HID:]
        weights = cw[:, pl.ds(pl.multiple_of((t * 2 + d) * ROWS, ROWS), ROWS), :].reshape(NY * ROWS, 128)
        lane = lax.broadcasted_iota(jnp.int32, weights.shape, 1)
        weight = jnp.sum(jnp.where(lane == r, weights, 0.0), axis=1, keepdims=True)
        hidden = g / (1.0 + jnp.exp(-g)) * u * weight
        hid[d, :, pl.ds(pl.multiple_of(r * HID, HID), HID)] = hidden.astype(BF16)

    def down(d, c):
        part[d, :, cols(c)] = jnp.dot(hid[d], wd[:, cols(c)], preferred_element_type=F32)

    def scatter(t, d, c):
        ring = []
        for h in range(4):
            if h == 0:
                ring.append((
                    copy_to(snd.at[t, d, pl.ds(0, HALF), cols(c)], rsb.at[t, d, 0, 0, pl.ds(0, HALF), cols(c)], right),
                    copy_to(snd.at[t, d, pl.ds(HALF, HALF), cols(c)], rsb.at[t, d, 1, 0, pl.ds(HALF, HALF), cols(c)], left)))
            else:
                ring.append((
                    copy_to(rsb.at[t, d, 0, h - 1, :, cols(c)], rsb.at[t, d, 0, h, :, cols(c)], right),
                    copy_to(rsb.at[t, d, 1, h - 1, :, cols(c)], rsb.at[t, d, 1, h, :, cols(c)], left)))
        return ring

    rs = [[[scatter(t, d, c) for c in range(NC)] for d in range(2)] for t in range(2)]

    def rs_hop(t, d, c, h):
        ring = rs[t][d][c]
        if h == 0:
            snd[t, d, :, cols(c)] = part[d, slot(4), cols(c)].astype(BF16)
            ring[0][0].start()
            ring[0][1].start()
            return
        for side in range(2):
            mine = (4 + h) if side == 0 else (4 - h)
            ring[h - 1][side].wait_recv()
            buf = rsb.at[t, d, side, h - 1]
            if h == 1:
                both, lone = (0, 1) if side == 0 else (1, 0)
                at = pl.ds(both * HALF, HALF)
                buf[at, cols(c)] = (buf[at, cols(c)].astype(F32) + part[d, slot(mine, both), cols(c)]).astype(BF16)
                buf[pl.ds(lone * HALF, HALF), cols(c)] = part[d, slot(mine, lone), cols(c)].astype(BF16)
            else:
                buf[:, cols(c)] = (buf[:, cols(c)].astype(F32) + part[d, slot(mine), cols(c)]).astype(BF16)
            ring[h][side].start()

    def rs_sum(t, d, c, x):
        rs[t][d][c][3][0].wait_recv()
        rs[t][d][c][3][1].wait_recv()
        mixed = (part[d, slot(0), cols(c)] + rsb[t, d, 0, 3, :, cols(c)].astype(F32)
                 + rsb[t, d, 1, 3, :, cols(c)].astype(F32))
        return (x.astype(F32) + mixed).astype(BF16)

    shift = [[copy_to(xs.at[d, :, cols(c)], xin.at[d, :, cols(c)], onward if d == 0 else backward)
              for c in range(NC)] for d in range(2)]

    def hand_on(d, c):
        xs[d, :, cols(c)] = rs_sum(0, d, c, state[d, 0, :, cols(c)])
        shift[d][c].start()

    def next_input(d):
        for c in range(NC):
            shift[d][c].wait_recv()

        @pl.when(section == (0 if d == 0 else n_section - 1))
        def _():
            xin[d] = fresh[d]

        xn[1, d, slot(0)] = normed(xin[d])

    def own_ready(q):
        own[q][0].wait()
        own[q][1].wait()

    for q in (0, 2, 1, 3):
        own_ready(q)
    gu_r[0].start()
    gu_l[2].start()
    ag_hop(0, 0, 0)
    ag_hop(0, 1, 0)
    gu_r[1].start()
    gu_l[3].start()
    own_wd.wait()
    ag_hop(0, 0, 1)
    ag_hop(0, 1, 1)
    gu_r[2].start()
    gu_l[0].start()
    ag_hop(0, 0, 2)
    ag_hop(0, 1, 2)
    gu_r[3].start()
    gu_l[1].start()
    ag_hop(0, 0, 3)
    ag_hop(0, 1, 3)
    cw_ring[0][0].start()
    cw_ring[0][1].start()
    gu_r[0].wait_recv()
    gu_fr[0].start()
    gu_l[2].wait_recv()
    gu_fl[2].start()
    ag_hop(0, 0, 4)
    ag_hop(0, 1, 4)
    for h in range(1, 5):
        for side in range(2):
            if cw_ring[h - 1][side] is not None:
                cw_ring[h - 1][side].wait_recv()
            if h < 4 and cw_ring[h][side] is not None:
                cw_ring[h][side].start()
    gu_r[1].wait_recv()
    gu_fr[1].start()
    gu_l[3].wait_recv()
    gu_fl[3].start()
    for c in (0, 1):
        wd_r[c].start()
        wd_l[c].start()

    def both(r):
        @pl.loop(0, 2)
        def _(d):
            gate_up(0, d, r)

    both(0)
    gu_r[2].wait_recv()
    gu_r[3].wait_recv()
    both(1)
    gu_l[0].wait_recv()
    gu_l[1].wait_recv()
    both(3)
    gu_fr[0].wait_recv()
    gu_fl[2].wait_recv()
    gu_fr[1].wait_recv()
    gu_fl[3].wait_recv()
    for c in (2, 3):
        wd_r[c].start()
        wd_l[c].start()
    wd_r[0].wait_recv()
    wd_fr[0].start()
    wd_l[0].wait_recv()
    wd_fl[0].start()
    both(2)

    for phase in range(2 * NC + 4):
        i, odd = phase // 2, phase % 2
        if odd == 0:
            if i < NC:
                if i + 1 < NC:
                    wd_r[i + 1].wait_recv()
                    wd_fr[i + 1].start()
                    wd_l[i + 1].wait_recv()
                    wd_fl[i + 1].start()
                wd_fr[i].wait_recv()
                wd_fl[i].wait_recv()
            for d in range(2):
                if 0 <= i - 2 < NC:
                    hand_on(d, i - 2)
                if 0 <= i - 1 < NC:
                    rs_hop(0, d, i - 1, 2)
                if i < NC:
                    down(d, i)
                    rs_hop(0, d, i, 0)
        else:
            for d in range(2):
                if 0 <= i - 1 < NC:
                    rs_hop(0, d, i - 1, 3)
                if i < NC:
                    rs_hop(0, d, i, 1)

    for d in range(2):
        next_input(d)
        ag_hop(1, d, 0)
    for h in range(1, 4):
        ag_hop(1, 0, h)
        ag_hop(1, 1, h)

    def experts(d):
        @pl.loop(0, NX)
        def _(r):
            gate_up(1, d, r)

    ag_hop(1, 0, 4)
    experts(0)
    for c in range(NC):
        down(0, c)
        rs_hop(1, 0, c, 0)
    ag_hop(1, 1, 4)
    for c in range(NC):
        rs_hop(1, 0, c, 1)
    experts(1)
    for c in range(NC):
        rs_hop(1, 0, c, 2)
    for c in range(NC):
        down(1, c)
        rs_hop(1, 1, c, 0)
    for c in range(NC):
        rs_hop(1, 0, c, 3)
    for c in range(NC):
        rs_hop(1, 1, c, 1)
    for c in range(NC):
        out[0, 0, :, cols(c)] = rs_sum(1, 0, c, xin[0, :, cols(c)])
    for h in (2, 3):
        for c in range(NC):
            rs_hop(1, 1, c, h)
    for c in range(NC):
        out[1, 0, :, cols(c)] = rs_sum(1, 1, c, xin[1, :, cols(c)])

    for copy in sent:
        copy.wait_send()


def solution(mesh):
    n_section = mesh.shape["section"]

    def per_device(state, fresh, norm_gain, w_gate, w_up, w_down, routes, gates):
        vmem = pl.BlockSpec(memory_space=pltpu.VMEM)
        hbm = pl.BlockSpec(memory_space=pl.ANY)
        return pl.pallas_call(
            functools.partial(kernel, n_section),
            out_shape=jax.ShapeDtypeStruct(state.shape, state.dtype),
            in_specs=[vmem, vmem, vmem, hbm, hbm, hbm, vmem, vmem],
            out_specs=vmem,
            scratch_shapes=[
                pltpu.VMEM((NX, D, 2 * HID), BF16),
                pltpu.VMEM((NX * HID, D), BF16),
                pltpu.VMEM((2, 2, NY * ROWS, D), BF16),
                pltpu.VMEM((2, NY * ROWS, NX * HID), BF16),
                pltpu.VMEM((2, NY * ROWS, D), F32),
                pltpu.VMEM((2, 2, 2, 4, ROWS, D), BF16),
                pltpu.VMEM((2, 2, ROWS, D), BF16),
                pltpu.VMEM((2, ROWS, D), BF16),
                pltpu.VMEM((2, ROWS, D), BF16),
                pltpu.VMEM((NY, 4 * ROWS, 128), F32),
                pltpu.SemaphoreType.DMA((N_SEMS,)),
                pltpu.SemaphoreType.DMA((N_SEMS,)),
                pltpu.SemaphoreType.DMA((2 * NQ + 1,)),
            ],
            compiler_params=pltpu.CompilerParams(
                collective_id=0, has_side_effects=True, vmem_limit_bytes=58 * 2**20),
        )(state, fresh, norm_gain, w_gate, w_up, w_down, routes, gates)

    rows = P(None, "section", "expert", None)
    named = P(None, None, "section", "expert", None)
    return jax.shard_map(
        per_device, mesh=mesh,
        in_specs=(rows, P(None, "expert", None), P("section", None), P("section", None, "expert"),
                  P("section", None, "expert"), P("section", "expert", None), named, named),
        out_specs=rows, check_vma=False)
```

time: 1110 us -> 220 us (0.20)
  the two profiles are of different devices: /device:TPU:249 before, /device:TPU:8 now
where the time goes in v1:
time: 220 us
  Pallas kernels  216 us (98%)
  local copies, waits for them, and re-layouts  3.98 us (2%)
    pallas_call x1, Pallas kernels, per_device(): pl.pallas_call(functools.partial(kernel, n_section), out_shape=jax.ShapeD...  216 us

profile of v1, /device:TPU:8, one launch (start us, length us, event | category | flops | bytes accessed | tf_op | source)
XLA Modules:
  0.0 220.0 jit_solution(1120738112497462791)
XLA Ops:
  0.0 0.0 copy-start
  0.0 1.4 copy.9.routes
  1.4 0.0 copy-done
  1.4 0.7 copy.10.gates
  2.2 216.1 %shard_map.82 = bf16[2,1,32,3584]{3,2,1,0:T(8,128)(2,1)} custom-call(bf16[2,1,32,3584]{3,2,1,0:T(8,128)(2,1)} %state.1, bf16[2,32,3584]{2,1,0:T(8,128)(2,1)} %fresh.1, f32[1,3584]{1,0:T(1,128)} %gain.1, bf16[1,3584,128]{2,1,0:T(8,128)(2,1)} %w_gate.1, bf16[1,3584,128]{2,1,0:T(8,128)(2,1)} %w_up.1, bf16[1,128,3584]{2,1,0:T(8,128)(2,1)} %w_down.1, ...), custom_call_target="tpu_custom_call" | custom-call | tf_op jit(solution)/shard_map/pallas_call | solution.py:346
  218.2 1.8 copy.12
Async XLA Ops:
  0.0 1.4 copy-start

commit v2 on v0

v2 whole, which is shorter than its diff:
```python
import functools

import jax
import jax.numpy as jnp
from jax import lax
from jax.experimental import pallas as pl
from jax.experimental.pallas import tpu as pltpu
from jax.sharding import PartitionSpec as P

MESH = pl.DeviceIdType.MESH
NX, NY = 4, 8
ROWS = 32
HALF = ROWS // 2
D = 3584
HID = 128
NC = (7, 4)
COLS = (D // NC[0], D // NC[1])
QROWS = D // 2
N_SEMS = 320
F32, BF16 = jnp.float32, jnp.bfloat16


def kernel(n_section, state, fresh, gain, w_gate, w_up, w_down, routes, gates, out,
           wgu, wd, xn, hid, part, rsb, snd, xs, xin, cw, send_sem, recv_sem, local_sem):
    expert = lax.axis_index("expert")
    section = lax.axis_index("section")
    ix, iy = expert // NY, expert % NY

    def along(dx, dy):
        return {"expert": ((ix + dx + NX) % NX) * NY + (iy + dy + NY) % NY}

    right, left = along(0, 1), along(0, -1)
    x_right, x_left = along(1, 0), along(-1, 0)
    onward = {"section": (section + 1) % n_section}
    backward = {"section": (section + n_section - 1) % n_section}

    count = [0]
    sent = []

    def reserve(n):
        count[0] += n
        return count[0] - n

    def copy_to(src, dst, device, at=None):
        keep = at is None
        if keep:
            at = reserve(1)
        copy = pltpu.make_async_remote_copy(
            src_ref=src, dst_ref=dst, send_sem=send_sem.at[at], recv_sem=recv_sem.at[at],
            device_id=device, device_id_type=MESH)
        if keep:
            sent.append(copy)
        return copy

    barrier = pltpu.get_barrier_semaphore()
    for peer in (right, left, x_right, x_left, onward, backward):
        pl.semaphore_signal(barrier, inc=1, device_id=peer, device_id_type=MESH)

    own = [
        pltpu.make_async_copy(w_gate.at[0], wgu.at[0, :, pl.ds(0, HID)], local_sem.at[0]),
        pltpu.make_async_copy(w_up.at[0], wgu.at[0, :, pl.ds(HID, HID)], local_sem.at[1]),
        pltpu.make_async_copy(w_down.at[0], wd.at[pl.ds(0, HID)], local_sem.at[2])]

    def normed(x):
        wide = x.astype(F32)
        mean_sq = jnp.mean(wide * wide, axis=-1, keepdims=True)
        return (wide * lax.rsqrt(mean_sq + 1e-06) * gain[...]).astype(BF16)

    def slot(s, half=None):
        if half is None:
            return pl.ds(s * ROWS, ROWS)
        return pl.ds(s * ROWS + half * HALF, HALF)

    def q_rows(q):
        return pl.ds(q * QROWS, QROWS)

    def gu_own(q, r, device):
        return [copy_to(w.at[0, q_rows(q)], wgu.at[r, q_rows(q), pl.ds(k * HID, HID)], device)
                for k, w in enumerate((w_gate, w_up))]

    gu_r = [gu_own(q, 1, x_right) for q in range(2)]
    gu_l = [gu_own(q, 3, x_left) for q in range(2)]
    gu_fr = copy_to(wgu.at[1, q_rows(0)], wgu.at[2, q_rows(0)], x_right)
    gu_fl = copy_to(wgu.at[3, q_rows(1)], wgu.at[2, q_rows(1)], x_left)

    def cols(t, c):
        at = c * COLS[t]
        return pl.ds(at if isinstance(c, int) else pl.multiple_of(at, 128), COLS[t])

    def wd_at(r, c, half=None):
        if half is None:
            return wd.at[pl.ds(r * HID, HID), cols(0, c)]
        return wd.at[pl.ds(r * HID + half * (HID // 2), HID // 2), cols(0, c)]

    wd_sems = reserve(4 * NC[0])

    def wd_own(c):
        return (copy_to(w_down.at[0, :, cols(0, c)], wd_at(1, c), x_right, wd_sems + 4 * c),
                copy_to(w_down.at[0, :, cols(0, c)], wd_at(3, c), x_left, wd_sems + 4 * c + 1))

    def wd_on(c):
        return (copy_to(wd_at(1, c, 0), wd_at(2, c, 0), x_right, wd_sems + 4 * c + 2),
                copy_to(wd_at(3, c, 1), wd_at(2, c, 1), x_left, wd_sems + 4 * c + 3))

    def wd_pass(c):
        for came, on in zip(wd_own(c), wd_on(c)):
            came.wait_recv()
            on.start()

    def start(copies):
        for copy in copies:
            copy.start()

    def arrive(copies):
        for copy in copies:
            copy.wait_recv()

    def gather(t, d):
        ring = []
        for h in range(4):
            pieces = []
            for k in range(2):
                to_right = to_left = None
                if h < 3 or k == 0:
                    to_right = copy_to(xn.at[t, d, slot(h, k)], xn.at[t, d, slot(h + 1, k)], right)
                if h < 3 or k == 1:
                    to_left = copy_to(xn.at[t, d, slot((8 - h) % 8, k)], xn.at[t, d, slot(7 - h, k)], left)
                pieces.append((to_right, to_left))
            ring.append(pieces)
        return ring

    ag = [[gather(t, d) for d in range(2)] for t in range(2)]

    def ag_hop(t, d, h):
        for k in range(2):
            for side in range(2):
                if h > 0 and ag[t][d][h - 1][k][side] is not None:
                    ag[t][d][h - 1][k][side].wait_recv()
                if h < 4 and ag[t][d][h][k][side] is not None:
                    ag[t][d][h][k][side].start()

    cw_ring = [(copy_to(cw.at[h], cw.at[h + 1], right),
                copy_to(cw.at[(8 - h) % 8], cw.at[7 - h], left) if h < 3 else None) for h in range(4)]

    def cw_hop(h):
        for side in range(2):
            if h > 0 and cw_ring[h - 1][side] is not None:
                cw_ring[h - 1][side].wait_recv()
            if h < 4 and cw_ring[h][side] is not None:
                cw_ring[h][side].start()

    def combine_weights():
        column_expert = ((ix + NX - lax.broadcasted_iota(jnp.int32, (ROWS, 128), 1) % NX) % NX).astype(F32)
        eye = (lax.broadcasted_iota(jnp.int32, (ROWS, ROWS), 0)
               == lax.broadcasted_iota(jnp.int32, (ROWS, ROWS), 1))

        def column(row):
            return jnp.sum(jnp.where(eye, row, 0.0), axis=1, keepdims=True)

        for t in range(2):
            for d in range(2):
                ids, wts = routes[t, d, 0].astype(F32), gates[t, d, 0]
                cw[0, pl.ds((t * 2 + d) * ROWS, ROWS)] = (
                    jnp.where(column(ids[0:1]) == column_expert, column(wts[0:1]), 0.0)
                    + jnp.where(column(ids[1:2]) == column_expert, column(wts[1:2]), 0.0))

    def gate_up(t, d, r, first=0, last=NY):
        rows = pl.ds(first * ROWS, (last - first) * ROWS)
        joined = jnp.dot(xn[t, d, rows], wgu[r], preferred_element_type=F32)
        g, u = joined[:, :HID], joined[:, HID:]
        own_rows = pl.ds(pl.multiple_of((t * 2 + d) * ROWS, ROWS), ROWS)
        weights = cw[first:last, own_rows, :].reshape((last - first) * ROWS, 128)
        lane = lax.broadcasted_iota(jnp.int32, weights.shape, 1)
        weight = jnp.sum(jnp.where(lane == r, weights, 0.0), axis=1, keepdims=True)
        hidden = g / (1.0 + jnp.exp(-g)) * u * weight
        hid[d, rows, pl.ds(pl.multiple_of(r * HID, HID), HID)] = hidden.astype(BF16)

    def down(d, at):
        part[d, :, at] = jnp.dot(hid[d], wd[:, at], preferred_element_type=F32)

    rs_sems = [reserve(16 * n) for n in NC]

    def rs_copies(t, d, c, h):
        at = rs_sems[t] + ((d * NC[t] + c) * 4 + h) * 2
        if h == 0:
            return [copy_to(snd.at[t, d, pl.ds(k * HALF, HALF), cols(t, c)],
                            rsb.at[t, k, 0, d, pl.ds(k * HALF, HALF), cols(t, c)], (right, left)[k], at + k)
                    for k in range(2)]
        return [copy_to(rsb.at[t, k, h - 1, d, :, cols(t, c)], rsb.at[t, k, h, d, :, cols(t, c)],
                        (right, left)[k], at + k) for k in range(2)]

    def rs_hop(t, d, c, h):
        at_cols, onto = cols(t, c), rs_copies(t, d, c, h)
        if h == 0:
            snd[t, d, :, at_cols] = part[d, slot(4), at_cols].astype(BF16)
            start(onto)
            return
        came = rs_copies(t, d, c, h - 1)
        for side in range(2):
            mine = (4 + h) if side == 0 else (4 - h)
            came[side].wait_recv()
            buf = rsb.at[t, side, h - 1, d]
            if h == 1:
                at, lone = pl.ds(side * HALF, HALF), pl.ds((1 - side) * HALF, HALF)
                buf[at, at_cols] = (buf[at, at_cols].astype(F32) + part[d, slot(mine, side), at_cols]).astype(BF16)
                buf[lone, at_cols] = part[d, slot(mine, 1 - side), at_cols].astype(BF16)
            else:
                buf[:, at_cols] = (buf[:, at_cols].astype(F32) + part[d, slot(mine), at_cols]).astype(BF16)
            onto[side].start()

    def rs_sum(t, d, c, x):
        at_cols = cols(t, c)
        arrive(rs_copies(t, d, c, 3))
        mixed = (part[d, slot(0), at_cols] + rsb[t, 0, 3, d, :, at_cols].astype(F32)
                 + rsb[t, 1, 3, d, :, at_cols].astype(F32))
        return (x.astype(F32) + mixed).astype(BF16)

    shift_sems = reserve(2 * NC[0])

    def shift(d, c):
        return copy_to(xs.at[d, :, cols(0, c)], xin.at[d, :, cols(0, c)], {"section": (
            section + n_section + 1 - 2 * d) % n_section}, shift_sems + d * NC[0] + c)

    def hand_on(d, c):
        xs[d, :, cols(0, c)] = rs_sum(0, d, c, state[d, 0, :, cols(0, c)])
        shift(d, c).start()

    def next_input(d):
        for c in range(NC[0]):
            shift(d, c).wait_recv()

        @pl.when(section == (0 if d == 0 else n_section - 1))
        def _():
            xin[d] = fresh[d]

        xn[1, d, slot(0)] = normed(xin[d])

    pl.semaphore_wait(barrier, 6)
    start(gu_r[0])
    start(gu_l[1])
    start(gu_r[1])
    start(gu_l[0])
    for copy in own:
        copy.start()
    xn[0, 0, slot(0)] = normed(state[0, 0])
    ag_hop(0, 0, 0)
    xn[0, 1, slot(0)] = normed(state[1, 0])
    ag_hop(0, 1, 0)
    combine_weights()
    cw_hop(0)
    ag_hop(0, 0, 1)
    ag_hop(0, 1, 1)
    cw_hop(1)
    arrive(gu_r[0])
    gu_fr.start()
    arrive(gu_l[1])
    gu_fl.start()
    ag_hop(0, 0, 2)
    ag_hop(0, 1, 2)
    for c in (0, 1):
        start(wd_own(c))
    cw_hop(2)
    ag_hop(0, 0, 3)
    ag_hop(0, 1, 3)
    cw_hop(3)
    ag_hop(0, 0, 4)
    ag_hop(0, 1, 4)
    cw_hop(4)
    for copy in own:
        copy.wait()
    arrive(gu_r[1])
    arrive(gu_l[0])

    @pl.loop(0, 6)
    def _(j):
        gate_up(0, j % 2, j // 2 + j // 4)

    gu_fr.wait_recv()
    gu_fl.wait_recv()

    @pl.loop(0, 2)
    def _(d):
        gate_up(0, d, 2)

    wd_pass(0)
    start(wd_own(2))

    def back_hops(d, i):
        for h in (4, 3, 2, 1):
            if 0 <= i - h < NC[0]:
                if h == 4:
                    hand_on(d, i - h)
                else:
                    rs_hop(0, d, i - h, h)

    for i in range(NC[0] + 4):
        back_hops(0, i)
        if i + 1 < NC[0]:
            wd_pass(i + 1)
        if i + 3 < NC[0]:
            start(wd_own(i + 3))
        if i < NC[0]:
            arrive(wd_on(i))

            @pl.loop(0, 2)
            def _(d):
                down(d, cols(0, i))

            rs_hop(0, 0, i, 0)
        back_hops(1, i - 2)
        if 0 <= i - 2 < NC[0]:
            rs_hop(0, 1, i - 2, 0)

    back_hops(1, NC[0] + 2)
    next_input(0)
    ag_hop(1, 0, 0)
    back_hops(1, NC[0] + 3)
    ag_hop(1, 0, 1)
    next_input(1)
    ag_hop(1, 1, 0)
    ag_hop(1, 0, 2)
    ag_hop(1, 1, 1)
    ag_hop(1, 0, 3)

    def experts(d, half):
        @pl.loop(0, NX)
        def _(r):
            gate_up(1, d, r, half * NY // 2, (half + 1) * NY // 2)

    def all_down(d):
        @pl.loop(0, D // 512)
        def _(c):
            down(d, pl.ds(pl.multiple_of(c * 512, 512), 512))

    def hop_all(d, h):
        for c in range(NC[1]):
            if h < 4:
                rs_hop(1, d, c, h)
            else:
                out[d, 0, :, cols(1, c)] = rs_sum(1, d, c, xin[d, :, cols(1, c)])

    experts(0, 0)
    ag_hop(1, 1, 2)
    ag_hop(1, 0, 4)
    experts(0, 1)
    ag_hop(1, 1, 3)
    all_down(0)
    hop_all(0, 0)
    experts(1, 0)
    ag_hop(1, 1, 4)
    hop_all(0, 1)
    experts(1, 1)
    hop_all(0, 2)
    all_down(1)
    hop_all(1, 0)
    hop_all(0, 3)
    hop_all(1, 1)
    hop_all(0, 4)
    for h in range(2, 5):
        hop_all(1, h)

    for c in range(NC[0]):
        for h in range(4):
            for copy in rs_copies(0, 0, c, h) + rs_copies(0, 1, c, h):
                copy.wait_send()
        for copy in (shift(0, c), shift(1, c)) + wd_own(c) + wd_on(c):
            copy.wait_send()
    for d in range(2):
        for c in range(NC[1]):
            for h in range(4):
                for copy in rs_copies(1, d, c, h):
                    copy.wait_send()
    for copy in sent:
        copy.wait_send()


def solution(mesh):
    n_section = mesh.shape["section"]

    def per_device(state, fresh, norm_gain, w_gate, w_up, w_down, routes, gates):
        vmem = pl.BlockSpec(memory_space=pltpu.VMEM)
        hbm = pl.BlockSpec(memory_space=pl.ANY)
        return pl.pallas_call(
            functools.partial(kernel, n_section),
            out_shape=jax.ShapeDtypeStruct(state.shape, state.dtype),
            in_specs=[vmem, vmem, vmem, hbm, hbm, hbm, vmem, vmem],
            out_specs=vmem,
            scratch_shapes=[
                pltpu.VMEM((NX, D, 2 * HID), BF16),
                pltpu.VMEM((NX * HID, D), BF16),
                pltpu.VMEM((2, 2, NY * ROWS, D), BF16),
                pltpu.VMEM((2, NY * ROWS, NX * HID), BF16),
                pltpu.VMEM((2, NY * ROWS, D), F32),
                pltpu.VMEM((2, 2, 4, 2, ROWS, D), BF16),
                pltpu.VMEM((2, 2, ROWS, D), BF16),
                pltpu.VMEM((2, ROWS, D), BF16),
                pltpu.VMEM((2, ROWS, D), BF16),
                pltpu.VMEM((NY, 4 * ROWS, 128), F32),
                pltpu.SemaphoreType.DMA((N_SEMS,)),
                pltpu.SemaphoreType.DMA((N_SEMS,)),
                pltpu.SemaphoreType.DMA((3,)),
            ],
            compiler_params=pltpu.CompilerParams(
                collective_id=0, has_side_effects=True, vmem_limit_bytes=58 * 2**20),
        )(state, fresh, norm_gain, w_gate, w_up, w_down, jnp.swapaxes(routes, 3, 4), jnp.swapaxes(gates, 3, 4))

    rows = P(None, "section", "expert", None)
    named = P(None, None, "section", "expert", None)
    return jax.shard_map(
        per_device, mesh=mesh,
        in_specs=(rows, P(None, "expert", None), P("section", None), P("section", None, "expert"),
                  P("section", None, "expert"), P("section", "expert", None), named, named),
        out_specs=rows, check_vma=False)
```

time: 1110 us -> 208 us (0.19)
  the two profiles are of different devices: /device:TPU:249 before, /device:TPU:16 now
where the time goes in v2:
time: 208 us
  Pallas kernels  206 us (99%)
    pallas_call x1, Pallas kernels, per_device(): pl.pallas_call(functools.partial(kernel, n_section), out_shape=jax.ShapeD...  206 us

profile of v2, /device:TPU:16, one launch (start us, length us, event | category | flops | bytes accessed | tf_op | source)
XLA Modules:
  0.0 208.2 jit_solution(4863774047585803006)
XLA Ops:
  0.0 206.3 %shard_map.82 = bf16[2,1,32,3584]{3,2,1,0:T(8,128)(2,1)} custom-call(bf16[2,1,32,3584]{3,2,1,0:T(8,128)(2,1)} %state.1, bf16[2,32,3584]{2,1,0:T(8,128)(2,1)} %fresh.1, f32[1,3584]{1,0:T(1,128)} %gain.1, bf16[1,3584,128]{2,1,0:T(8,128)(2,1)} %w_gate.1, bf16[1,3584,128]{2,1,0:T(8,128)(2,1)} %w_up.1, bf16[1,128,3584]{2,1,0:T(8,128)(2,1)} %w_down.1, ...), custom_call_target="tpu_custom_call" | custom-call | tf_op jit(solution)/shard_map/pallas_call | solution.py:383
  206.3 1.8 copy.10

commit v3 on v2

--- a/solution.py
+++ b/solution.py
@@ -284,6 +284,8 @@
 
     wd_pass(0)
     start(wd_own(2))
+    wd_pass(1)
+    start(wd_own(3))
 
     def back_hops(d, i):
         for h in (4, 3, 2, 1):
@@ -295,10 +297,6 @@
 
     for i in range(NC[0] + 4):
         back_hops(0, i)
-        if i + 1 < NC[0]:
-            wd_pass(i + 1)
-        if i + 3 < NC[0]:
-            start(wd_own(i + 3))
         if i < NC[0]:
             arrive(wd_on(i))
 
@@ -307,6 +305,10 @@
                 down(d, cols(0, i))
 
             rs_hop(0, 0, i, 0)
+        if i + 2 < NC[0]:
+            wd_pass(i + 2)
+        if i + 4 < NC[0]:
+            start(wd_own(i + 4))
         back_hops(1, i - 2)
         if 0 <= i - 2 < NC[0]:
             rs_hop(0, 1, i - 2, 0)

time: 208 us -> 209 us (level)
  no operation moved by 1% of the time
where the time goes in v3:
time: 209 us
  Pallas kernels  207 us (99%)
    pallas_call x1, Pallas kernels, per_device(): pl.pallas_call(functools.partial(kernel, n_section), out_shape=jax.ShapeD...  207 us

profile of v3, /device:TPU:16, one launch (start us, length us, event | category | flops | bytes accessed | tf_op | source)
XLA Modules:
  0.0 208.8 jit_solution(17201306148811445025)
XLA Ops:
  0.0 207.0 %shard_map.82 = bf16[2,1,32,3584]{3,2,1,0:T(8,128)(2,1)} custom-call(bf16[2,1,32,3584]{3,2,1,0:T(8,128)(2,1)} %state.1, bf16[2,32,3584]{2,1,0:T(8,128)(2,1)} %fresh.1, f32[1,3584]{1,0:T(1,128)} %gain.1, bf16[1,3584,128]{2,1,0:T(8,128)(2,1)} %w_gate.1, bf16[1,3584,128]{2,1,0:T(8,128)(2,1)} %w_up.1, bf16[1,128,3584]{2,1,0:T(8,128)(2,1)} %w_down.1, ...), custom_call_target="tpu_custom_call" | custom-call | tf_op jit(solution)/shard_map/pallas_call | solution.py:385
  207.0 1.8 copy.10
